TPU v7x, 128 devices: a whole 4x4x4 slice. The times are simulated.
128 devices in a mesh: dp: 4 (over x_hi, core), section: 2 (over x_lo), seq: 16 (over z, y).
Axes of the slice: x: 4 (x_hi: 2, x_lo: 2; x = x_hi * 2 + x_lo), y: 4, z: 4, core: 2. Of those that a mesh axis runs over, the one named last changes fastest.
Arguments:
- streams: bfloat16 [2, 4, 2048, 1152], P('section', 'dp', 'seq'), may hold values from -30 to 30
- modulation: float32 [2, 2, 3, 1152], P('section'), may hold values from -2 to 2, as said below
- w_qkv: bfloat16 [2, 2, 16, 3, 72, 1152], P('section', None, 'seq'), may hold values from -2 to 2
- w_out: bfloat16 [2, 2, 16, 72, 1152], P('section', None, 'seq'), may hold values from -0.1875 to 0.1875
- w_zero: bfloat16 [2, 1152, 1152], replicated, may hold values from -0.1875 to 0.1875
- pairing: int32 [4, 2], P('dp'), may hold values from 0 to 1, as said below
- positions: int32 [2048], P('seq'), may hold values from 0 to 2047, each once
- cotangent: bfloat16 [4, 2048, 1152], P('dp', 'seq'), may hold values from -0.59765625 to 0.59765625
Outputs:
- final: bfloat16 [2, 4, 2048, 1152], P('section', 'dp', 'seq')
- stream_grads: float32 [2, 4, 2048, 1152], P('section', 'dp', 'seq')
- grad_qkv: float32 [2, 2, 16, 3, 72, 1152], P('section', None, 'seq')
- grad_out: float32 [2, 2, 16, 72, 1152], P('section', None, 'seq')
Inputs may be any that keep to these rules, and one draw needn't show every extreme that they name: `modulation`: entries 0, 1, 2 of the third dimension are shift, scale and gate; gates are positive. pairing[b, j] >= j for every sequence b and control block j.
All inputs are finite; a program needn't handle non-finite values.
Results may differ from a plain program's by a relative error of at most 0.03.
Values may be sent and summed in bfloat16 or wider, within the bound.
No kernel may reach another device: no remote copies, remote signals or barrier semaphores. Data moves between devices by JAX's collectives and lax.ppermute only.
A program may use at most 192 MiB of HBM per device.

v0:
```python
import math

import jax
import jax.numpy as jnp
from jax import lax
from jax.sharding import PartitionSpec as P

GRID_W = 128


norm_eps = 1e-06


def shifted(value, axis, by):
    count = lax.axis_size(axis)
    pairs = [(i, i + by) for i in range(count) if 0 <= i + by < count]
    return lax.ppermute(value, axis, pairs)


def angle_tables(places, head_size):
    quarter = head_size // 4
    grid_rows = (places // GRID_W).astype(jnp.float32)
    grid_cols = (places % GRID_W).astype(jnp.float32)
    freqs = jnp.exp(-math.log(10000.0) * jnp.arange(quarter, dtype=jnp.float32) / quarter)
    row_angle = grid_rows[:, None] * freqs[None, :]
    col_angle = grid_cols[:, None] * freqs[None, :]
    return (jnp.cos(row_angle), jnp.sin(row_angle), jnp.cos(col_angle), jnp.sin(col_angle))


def expand(table_in, rank_count):
    return table_in.reshape(table_in.shape[:1] + (1,) * (rank_count - 2) + table_in.shape[1:])


def turn_half(part_vals, cosine, sine_tab):
    quarter = cosine.shape[1]
    cosine = expand(cosine, part_vals.ndim)
    sine_tab = expand(sine_tab, part_vals.ndim)
    first_half = part_vals[..., :quarter]
    second_half = part_vals[..., quarter:]
    return jnp.concatenate(
        [
            first_half * cosine - second_half * sine_tab,
            first_half * sine_tab + second_half * cosine,
        ],
        axis=-1,
    )


def rotate(values, tables):
    middle = values.shape[-1] // 2
    return jnp.concatenate(
        [
            turn_half(values[..., :middle], tables[0], tables[1]),
            turn_half(values[..., middle:], tables[2], tables[3]),
        ],
        axis=-1,
    )


def unrotate(values, tables):
    return rotate(values, (tables[0], -tables[1], tables[2], -tables[3]))


def rope_qkv(raw_proj, tables):
    turned = rotate(raw_proj[:, :, :2], tables)
    return jnp.concatenate([turned, raw_proj[:, :, 2:]], axis=2).astype(jnp.bfloat16)


def attend_head(head_qkv):
    head_size = head_qkv.shape[2]
    scores = lax.dot_general(
        head_qkv[:, 0], head_qkv[:, 1], (((1,), (1,)), ((), ())), preferred_element_type=jnp.float32
    ) / math.sqrt(head_size)
    weights = jax.nn.softmax(scores, axis=-1).astype(jnp.bfloat16)
    return jnp.dot(weights, head_qkv[:, 2], preferred_element_type=jnp.float32).astype(jnp.bfloat16)


def back_head(head_qkv, grad_heads, tables):
    head_size = head_qkv.shape[2]
    query = head_qkv[:, 0]
    keys_in = head_qkv[:, 1]
    values_in = head_qkv[:, 2]
    scores = lax.dot_general(
        query, keys_in, (((1,), (1,)), ((), ())), preferred_element_type=jnp.float32
    ) / math.sqrt(head_size)
    probs = jax.nn.softmax(scores, axis=-1)
    grad_values = lax.dot_general(
        probs.astype(jnp.bfloat16),
        grad_heads,
        (((0,), (0,)), ((), ())),
        preferred_element_type=jnp.float32,
    )
    grad_probs = lax.dot_general(
        grad_heads, values_in, (((1,), (1,)), ((), ())), preferred_element_type=jnp.float32
    )
    centred = grad_probs - jnp.sum(probs * grad_probs, axis=-1, keepdims=True)
    grad_scores = (probs * centred / math.sqrt(head_size)).astype(jnp.bfloat16)
    grad_query = jnp.dot(grad_scores, keys_in, preferred_element_type=jnp.float32)
    grad_keys = lax.dot_general(
        grad_scores, query, (((0,), (0,)), ((), ())), preferred_element_type=jnp.float32
    )
    return jnp.stack(
        [unrotate(grad_query, tables), unrotate(grad_keys, tables), grad_values], axis=1
    )


def modulated_norm(hidden, shift_vec, scale_vec):
    centre = hidden - jnp.mean(hidden, axis=-1, keepdims=True)
    spread = jnp.mean(centre * centre, axis=-1, keepdims=True)
    return centre * lax.rsqrt(spread + norm_eps) * (1.0 + scale_vec) + shift_vec


def local(streams, modulation, w_qkv, w_out, w_zero, pairing, positions, cotangent):
    section_pos = lax.axis_index("section")
    hidden = streams[0, 0].astype(jnp.float32)
    mod_own = modulation[0]
    qkv_own = w_qkv[0]
    blocks = qkv_own.shape[0]
    heads_here = qkv_own.shape[1]
    head_size = qkv_own.shape[3]
    width = qkv_own.shape[4]
    pair_row = pairing[0]
    qkv_rows = qkv_own.reshape(blocks, heads_here * 3 * head_size, width)
    out_rows = w_out[0].reshape(blocks, heads_here * head_size, width)
    tables = angle_tables(lax.all_gather(positions, "seq", axis=0, tiled=True), head_size)
    length = tables[0].shape[0]
    kept_state = []
    received = []
    for block_index in range(blocks):
        shift_vec = mod_own[block_index, 0]
        scale_vec = mod_own[block_index, 1]
        gate_vec = mod_own[block_index, 2]
        normed = modulated_norm(hidden, shift_vec, scale_vec).astype(jnp.bfloat16)
        gathered = lax.all_gather(normed, "seq", axis=0, tiled=True)
        raw_proj = lax.dot_general(
            gathered,
            qkv_rows[block_index],
            (((1,), (1,)), ((), ())),
            preferred_element_type=jnp.float32,
        )
        qkv_rot = rope_qkv(raw_proj.reshape(length, heads_here, 3, head_size), tables)
        head_outs = lax.map(attend_head, jnp.moveaxis(qkv_rot, 1, 0))
        mixed_heads = jnp.moveaxis(head_outs, 0, 1).reshape(length, heads_here * head_size)
        regrouped = mixed_heads
        attn_sum = lax.psum_scatter(
            jnp.dot(mixed_heads, out_rows[block_index], preferred_element_type=jnp.float32).astype(
                jnp.bfloat16
            ),
            "seq",
            scatter_dimension=0,
            tiled=True,
        ).astype(jnp.float32)
        kept_state.append((hidden, gathered, qkv_rot, regrouped))
        hidden = hidden + gate_vec * attn_sum
        control_out = jnp.dot(
            hidden.astype(jnp.bfloat16), w_zero[block_index], preferred_element_type=jnp.float32
        ).astype(jnp.bfloat16)
        received.append(shifted(control_out, "section", 1))
        for earlier in range(block_index + 1):
            hidden = hidden + jnp.where(
                pair_row[earlier] == block_index, received[earlier].astype(jnp.float32), 0.0
            )
    final_out = hidden.astype(jnp.bfloat16)[None, None]
    grad_flow = jnp.where(section_pos == 1, cotangent[0].astype(jnp.float32), 0.0)
    sent_back = [None] * blocks
    qkv_grads = [None] * blocks
    out_grads = [None] * blocks
    for block_index in reversed(range(blocks)):
        sent_back[block_index] = shifted(grad_flow.astype(jnp.bfloat16), "section", -1)
        picked = jnp.zeros_like(grad_flow)
        for later_block in range(block_index, blocks):
            picked = picked + jnp.where(
                pair_row[block_index] == later_block,
                sent_back[later_block].astype(jnp.float32),
                0.0,
            )
        grad_flow = grad_flow + lax.dot_general(
            picked.astype(jnp.bfloat16),
            w_zero[block_index],
            (((1,), (1,)), ((), ())),
            preferred_element_type=jnp.float32,
        )
        hidden_in, gathered, qkv_rot, regrouped = kept_state[block_index]
        shift_vec = mod_own[block_index, 0]
        scale_vec = mod_own[block_index, 1]
        gate_vec = mod_own[block_index, 2]
        d_attn = (gate_vec * grad_flow).astype(jnp.bfloat16)
        d_full = lax.all_gather(d_attn, "seq", axis=0, tiled=True)
        d_mixed = lax.dot_general(
            d_full,
            out_rows[block_index],
            (((1,), (1,)), ((), ())),
            preferred_element_type=jnp.float32,
        ).astype(jnp.bfloat16)
        grad_out_w = lax.dot_general(
            regrouped, d_full, (((0,), (0,)), ((), ())), preferred_element_type=jnp.float32
        )
        head_grads = lax.map(
            lambda pair_in: back_head(pair_in[0], pair_in[1], tables),
            (
                jnp.moveaxis(qkv_rot, 1, 0),
                jnp.moveaxis(d_mixed.reshape(length, heads_here, head_size), 1, 0),
            ),
        )
        d_raw = (
            jnp.moveaxis(head_grads, 0, 1)
            .reshape(length, heads_here * 3 * head_size)
            .astype(jnp.bfloat16)
        )
        grad_qkv_w = lax.dot_general(
            d_raw, gathered, (((0,), (0,)), ((), ())), preferred_element_type=jnp.float32
        )
        d_normed = lax.psum_scatter(
            jnp.dot(d_raw, qkv_rows[block_index], preferred_element_type=jnp.float32).astype(
                jnp.bfloat16
            ),
            "seq",
            scatter_dimension=0,
            tiled=True,
        ).astype(jnp.float32)
        norm_back = jax.vjp(lambda inner: modulated_norm(inner, shift_vec, scale_vec), hidden_in)[
            1
        ](d_normed)[0]
        grad_flow = grad_flow + norm_back
        qkv_grads[block_index] = grad_qkv_w
        out_grads[block_index] = grad_out_w
    qkv_total, out_total = (
        lax.psum(jnp.stack(qkv_grads).astype(jnp.bfloat16), "dp").astype(jnp.float32),
        lax.psum(jnp.stack(out_grads).astype(jnp.bfloat16), "dp").astype(jnp.float32),
    )
    grad_qkv = qkv_total.reshape(blocks, heads_here, 3, head_size, width)[None]
    grad_out = out_total.reshape(blocks, heads_here, head_size, width)[None]
    return (final_out, grad_flow[None, None], grad_qkv, grad_out)


def solution(mesh):
    in_specs = (
        P("section", "dp", "seq", None),
        P("section", None, None, None),
        P("section", None, "seq", None, None, None),
        P("section", None, "seq", None, None),
        P(),
        P("dp", None),
        P("seq"),
        P("dp", "seq", None),
    )
    out_specs = (
        P("section", "dp", "seq", None),
        P("section", "dp", "seq", None),
        P("section", None, "seq", None, None, None),
        P("section", None, "seq", None, None),
    )
    return jax.shard_map(local, mesh=mesh, in_specs=in_specs, out_specs=out_specs, check_vma=False)
```

profile of v0, /device:TPU:0, one launch (start us, length us, event | category | flops | bytes accessed | tf_op | source)
XLA Modules:
  0.0 741.6 jit_solution(12785375285632239583)
XLA Ops:
  13.6 22.2 %all-gather = s32[16,1,128]{2,1,0:T(1,128)S(1)} all-gather(s32[1,1,128]{2,1,0:T(1,128)} %bitcast.210), channel_id=1, replica_groups=mesh['dp'=4,'section'=2,'seq'=16] {'seq'}, dimensions={0}, use_global_device_ids=true | all-gather | bytes 8704 | tf_op jit(solution)/shard_map/all_gather | solution.py:125
  37.8 32.5 %all-gather.6.cloned.1.call-done = bf16[2048,1152]{1,0:T(8,128)(2,1)} async-done(((bf16[128,1152]{1,0:T(8,128)(2,1)}), bf16[2048,1152]{1,0:T(8,128)(2,1)}) %all-gather.6.cloned.1.call-update) | async-done | bytes 4718608 | tf_op jit(solution)/shard_map/all_gather | solution.py:134
  70.3 4.1 fusion.24
  75.8 8.1 %multiply_reduce_fusion.3 = (f32[2048]{0:T(1024)S(1)}, f32[2048,2048]{0,1:T(8,128)}) fusion(bf16[2048,2,72]{0,2,1:T(8,128)(2,1)S(1)} %maximum_bitcast_fusion), kind=kOutput, calls=%fused_computation.7 | convolution fusion | flops 612366336 | bytes 17375232 | tf_op jit(solution)/shard_map/while/body/eval_jaxpr/dot_general | solution.py:71
  83.9 8.6 %fusion.1 = f32[2048]{0:T(1024)S(1)} fusion(f32[2048,2048]{0,1:T(8,128)} %get-tuple-element.150, f32[2048]{0:T(1024)S(1)} %get-tuple-element.149), kind=kLoop, calls=%fused_computation.9 | loop fusion | flops 12580864 | bytes 16793600 | tf_op jit(solution)/shard_map/while/body/eval_jaxpr/reduce_sum | solution.py:74
  92.5 7.7 %fusion.54 = bf16[2048,72]{0,1:T(8,128)(2,1)S(1)} fusion(f32[2048,1,3,72]{0,3,2,1:T(8,128)S(1)} %fusion.24, f32[2048,2048]{0,1:T(8,128)} %get-tuple-element.150, f32[2048]{0:T(1024)S(1)} %fusion.1, f32[2048]{0:T(1024)S(1)} %get-tuple-element.149), kind=kOutput, calls=%fused_computation.56 | convolution fusion | flops 620904448 | bytes 17383424 | tf_op jit(solution)/shard_map/while/body/eval_jaxpr/dot_general | solution.py:75
  100.9 3.6 convolution_convert_fusion.3
  107.6 7.7 %collective-permute-done.2 = bf16[128,1152]{1,0:T(8,128)(2,1)S(1)} collective-permute-done((bf16[128,1152]{1,0:T(8,128)(2,1)S(1)}, bf16[128,1152]{1,0:T(8,128)(2,1)S(1)}, u32[]{:S(2)}, u32[]{:S(2)}) %collective-permute-start.2) | collective-permute-done | bytes 294944 | tf_op jit(solution)/shard_map/ppermute | solution.py:17
  115.3 3.5 multiply_convert_fusion.3
  118.9 64.0 %reduce-scatter.5.cloned.1.call-done = bf16[128,1152]{1,0:T(8,128)(2,1)} async-done(((bf16[2048,1152]{1,0:T(8,128)(2,1)}), bf16[128,1152]{1,0:T(8,128)(2,1)}) %reduce-scatter.5.cloned.1.call-update) | async-done | bytes 294928 | tf_op jit(solution)/shard_map/reduce_scatter | solution.py:145
  182.9 2.5 fusion.38
  185.4 3.4 collective-permute-start
  189.4 4.1 collective-permute-done
  195.9 2.0 fusion.171
  198.0 41.1 %all-gather.10.cloned.1.call-done = bf16[2048,1152]{1,0:T(8,128)(2,1)} async-done(((bf16[128,1152]{1,0:T(8,128)(2,1)}), bf16[2048,1152]{1,0:T(8,128)(2,1)}) %all-gather.10.cloned.1.call-update) | async-done | bytes 4718608 | tf_op jit(solution)/shard_map/all_gather | solution.py:188
  239.0 4.7 convolution_convert_fusion.9
  243.8 51.5 %all-gather.8.cloned.1.call-done = bf16[2048,1152]{1,0:T(8,128)(2,1)} async-done(((bf16[128,1152]{1,0:T(8,128)(2,1)}), bf16[2048,1152]{1,0:T(8,128)(2,1)}) %all-gather.8.cloned.1.call-update) | async-done | bytes 4718608 | tf_op jit(solution)/shard_map/all_gather | solution.py:134
  295.3 4.1 fusion.27
  300.0 8.1 %multiply_reduce_fusion.2 = (f32[2048]{0:T(1024)S(1)}, f32[2048,2048]{0,1:T(8,128)}) fusion(bf16[2048,2,72]{0,2,1:T(8,128)(2,1)S(1)} %maximum_bitcast_fusion.1), kind=kOutput, calls=%fused_computation.6 | convolution fusion | flops 612366336 | bytes 17375232 | tf_op jit(solution)/shard_map/while/body/eval_jaxpr/dot_general | solution.py:71
  308.1 8.6 %fusion.3 = f32[2048]{0:T(1024)S(1)} fusion(f32[2048,2048]{0,1:T(8,128)} %get-tuple-element.152, f32[2048]{0:T(1024)S(1)} %get-tuple-element.151), kind=kLoop, calls=%fused_computation.11 | loop fusion | flops 12580864 | bytes 16793600 | tf_op jit(solution)/shard_map/while/body/eval_jaxpr/reduce_sum | solution.py:74
  316.6 7.7 %fusion.57 = bf16[2048,72]{0,1:T(8,128)(2,1)S(1)} fusion(f32[2048,1,3,72]{0,3,2,1:T(8,128)S(1)} %fusion.27, f32[2048,2048]{0,1:T(8,128)} %get-tuple-element.152, f32[2048]{0:T(1024)S(1)} %fusion.3, f32[2048]{0:T(1024)S(1)} %get-tuple-element.151), kind=kOutput, calls=%fused_computation.57 | convolution fusion | flops 620904448 | bytes 17383424 | tf_op jit(solution)/shard_map/while/body/eval_jaxpr/dot_general | solution.py:75
  324.3 3.6 convolution_convert_fusion.2
  328.2 11.4 %multiply_reduce_fusion.1 = (f32[2048]{0:T(1024)S(1)}, f32[2048,2048]{0,1:T(8,128)}) fusion(f32[2048]{0:T(1024)S(1)} %fusion.3, f32[2048]{0:T(1024)S(1)} %get-tuple-element.151, f32[2048,2048]{0,1:T(8,128)} %get-tuple-element.152, bf16[2048,72]{0,1:T(8,128)(2,1)S(1)} %copy-done.11, f32[2048,1,3,72]{0,3,2,1:T(8,128)} %copy-done.8), kind=kOutput, calls=%fused_computation.3 | convolution fusion | flops 624949248 | bytes 34168832 | tf_op jit(solution)/shard_map/while/body/eval_jaxpr/dot_general | solution.py:93
  339.6 13.4 %multiply_convert_fusion.1 = bf16[2048,2048]{0,1:T(8,128)(2,1)S(1)} fusion(f32[2048,2048]{0,1:T(8,128)} %get-tuple-element.154, f32[2048]{0:T(1024)S(1)} %get-tuple-element.153, f32[2048]{0:T(1024)S(1)} %fusion.3, f32[2048]{0:T(1024)S(1)} %get-tuple-element.151, f32[2048,2048]{0,1:T(8,128)} %get-tuple-element.152), kind=kLoop, calls=%fused_computation.2 | loop fusion | flops 29360128 | bytes 41967616 | tf_op jit(solution)/shard_map/while/body/eval_jaxpr/convert_element_type | solution.py:97
  353.1 2.7 fusion.118
  359.5 3.6 fusion.47
  363.3 3.8 convolution_convert_fusion.1
  367.7 38.4 %reduce-scatter.7.cloned.1.call-done = bf16[128,1152]{1,0:T(8,128)(2,1)} async-done(((bf16[2048,1152]{1,0:T(8,128)(2,1)}), bf16[128,1152]{1,0:T(8,128)(2,1)}) %reduce-scatter.7.cloned.1.call-update) | async-done | bytes 294928 | tf_op jit(solution)/shard_map/reduce_scatter | solution.py:145
  406.1 3.2 fusion.41
  409.3 3.6 collective-permute-start.1
  412.9 74.0 %reduce-scatter.9.cloned.1.call-done = bf16[128,1152]{1,0:T(8,128)(2,1)} async-done(((bf16[2048,1152]{1,0:T(8,128)(2,1)}), bf16[128,1152]{1,0:T(8,128)(2,1)}) %reduce-scatter.9.cloned.1.call-update) | async-done | bytes 294928 | tf_op jit(solution)/shard_map/reduce_scatter | solution.py:213
  488.1 2.1 fusion.168
  491.7 7.8 %collective-permute-done.3 = bf16[128,1152]{1,0:T(8,128)(2,1)S(1)} collective-permute-done((bf16[128,1152]{1,0:T(8,128)(2,1)S(1)}, bf16[128,1152]{1,0:T(8,128)(2,1)S(1)}, u32[]{:S(2)}, u32[]{:S(2)}) %collective-permute-start.3) | collective-permute-done | bytes 294944 | tf_op jit(solution)/shard_map/ppermute | solution.py:17
  499.4 3.7 multiply_convert_fusion.2
  503.2 3.3 fusion.61
  506.5 3.7 fusion.37
  510.2 46.4 %all-gather.12.cloned.1.call-done = bf16[2048,1152]{1,0:T(8,128)(2,1)} async-done(((bf16[128,1152]{1,0:T(8,128)(2,1)}), bf16[2048,1152]{1,0:T(8,128)(2,1)}) %all-gather.12.cloned.1.call-update) | async-done | bytes 4718608 | tf_op jit(solution)/shard_map/all_gather | solution.py:188
  556.6 4.2 convolution_convert_fusion.8
  560.8 7.8 %fusion.44 = bf16[2048,1,72]{0,2,1:T(8,128)(2,1)S(1)} fusion(bf16[2048,72]{0,1:T(8,128)(2,1)S(1)} %convolution_convert_fusion.8, f32[2048,2048]{0,1:T(8,128)} %get-tuple-element.150, f32[2048]{0:T(1024)S(1)} %copy-done.22, f32[2048]{0:T(1024)S(1)} %copy-done.20), kind=kOutput, calls=%fused_computation.46 | convolution fusion | flops 620756992 | bytes 17383424 | tf_op jit(solution)/shard_map/while/body/eval_jaxpr/dot_general | solution.py:87
  570.2 8.9 %multiply_reduce_fusion = (f32[2048]{0:T(1024)S(1)}, f32[2048,2048]{0,1:T(8,128)}) fusion(f32[2048]{0:T(1024)S(1)} %copy-done.22, f32[2048]{0:T(1024)S(1)} %copy-done.20, f32[2048,2048]{0,1:T(8,128)S(1)} %bitcast.198, bf16[2048,72]{0,1:T(8,128)(2,1)S(1)} %convolution_convert_fusion.8, f32[2048,1,3,72]{0,3,2,1:T(8,128)} %copy-done.7), kind=kOutput, calls=%fused_computation.1 | convolution fusion | flops 624949248 | bytes 34168832 | tf_op jit(solution)/shard_map/while/body/eval_jaxpr/dot_general | solution.py:93
  579.1 8.4 %multiply_convert_fusion = bf16[2048,2048]{0,1:T(8,128)(2,1)S(1)} fusion(f32[2048,2048]{0,1:T(8,128)} %get-tuple-element.158, f32[2048]{0:T(1024)S(1)} %get-tuple-element.157, f32[2048]{0:T(1024)S(1)} %copy-done.22, f32[2048]{0:T(1024)S(1)} %copy-done.20, f32[2048,2048]{0,1:T(8,128)S(1)} %bitcast.198), kind=kLoop, calls=%fused_computation | loop fusion | flops 29360128 | bytes 41967616 | tf_op jit(solution)/shard_map/while/body/eval_jaxpr/convert_element_type | solution.py:97
  587.6 2.7 fusion.115
  591.9 3.3 fusion.60
  601.0 3.8 convolution_convert_fusion
  604.8 43.3 %all-reduce.3.cloned.1.call-done = (bf16[1,2,1,3,72,1152]{5,4,3,2,1,0:T(8,128)(2,1)}, bf16[1,2,1,72,1152]{4,3,1,2,0:T(8,128)(2,1)}) async-done(((bf16[1,2,1,3,72,1152]{5,4,3,2,1,0:T(8,128)(2,1)}, bf16[1,2,1,72,1152]{4,3,1,2,0:T(8,128)(2,1)}), (bf16[1,2,1,3,72,1152]{5,4,3,2,1,0:T(8,128)(2,1)}, bf16[1,2,1,72,1152]{4,3,1,2,0:T(8,128)(2,1)})) %all-reduce.3.cloned.1.call-update) | async-done | bytes 1327120 | tf_op jit(solution)/shard_map/psum | solution.py:228
  648.1 2.6 broadcast_in_dim_reshape.13
  652.6 77.5 %reduce-scatter.11.cloned.1.call-done = bf16[128,1152]{1,0:T(8,128)(2,1)} async-done(((bf16[2048,1152]{1,0:T(8,128)(2,1)}), bf16[128,1152]{1,0:T(8,128)(2,1)}) %reduce-scatter.11.cloned.1.call-update) | async-done | bytes 294928 | tf_op jit(solution)/shard_map/reduce_scatter | solution.py:213
  732.6 2.1 add_bitcast_fusion
  (155 shorter events, 35.6 us)
Async XLA Ops:
  7.2 63.1 %all-gather.6.cloned.1.call-start = ((), (), s32[]{:S(2)}) async-start(), calls=%async_computation.4 | async-start | bytes 5013504 | tf_op jit(solution)/shard_map/all_gather | solution.py:134
  13.5 169.4 %reduce-scatter.5.cloned.1.call-start = ((), (), s32[]{:S(2)}) async-start(), calls=%async_computation.5 | async-start | bytes 5013504 | tf_op jit(solution)/shard_map/reduce_scatter | solution.py:145
  35.7 39.0 %copy-start.27 = (f32[18]{0:T(128)}, f32[18]{0:T(128)S(1)}, u32[]{:S(2)}) copy-start(f32[18]{0:T(128)S(1)} %multiply_exponential_fusion) | copy-start | bytes 220
  74.4 18.1 %copy-start.7 = (f32[2048,1,3,72]{0,3,2,1:T(8,128)}, f32[2048,1,3,72]{0,3,2,1:T(8,128)S(1)}, u32[]{:S(2)}) copy-start(f32[2048,1,3,72]{0,3,2,1:T(8,128)S(1)} %fusion.24) | copy-start | bytes 5308420
  83.9 16.3 %copy-start.19 = (f32[2048]{0:T(1024)}, f32[2048]{0:T(1024)S(1)}, u32[]{:S(2)}) copy-start(f32[2048]{0:T(1024)S(1)} %get-tuple-element.149) | copy-start | bytes 24580
  92.5 7.7 %copy-start.21 = (f32[2048]{0:T(1024)}, f32[2048]{0:T(1024)S(1)}, u32[]{:S(2)}) copy-start(f32[2048]{0:T(1024)S(1)} %fusion.1) | copy-start | bytes 24580
  92.5 8.4 %copy-start.9 = (bf16[1,2,1,72,1152]{4,3,2,1,0:T(8,128)(2,1)S(1)}, bf16[1,2,1,72,1152]{4,3,2,1,0:T(8,128)(2,1)}, u32[]{:S(2)}) copy-start(bf16[1,2,1,72,1152]{4,3,2,1,0:T(8,128)(2,1)} %param.11) | copy-start | bytes 995332
  100.9 5.4 copy-start.29
  100.9 82.0 %copy-start = (bf16[1,1,128,1152]{3,2,1,0:T(8,128)(2,1)S(1)}, bf16[1,1,128,1152]{3,2,1,0:T(8,128)(2,1)}, u32[]{:S(2)}) copy-start(bf16[1,1,128,1152]{3,2,1,0:T(8,128)(2,1)} %param.8) | copy-start | bytes 884740
  104.6 134.5 %all-gather.10.cloned.1.call-start = ((), (), s32[]{:S(2)}) async-start(), calls=%async_computation.8 | async-start | bytes 5013504 | tf_op jit(solution)/shard_map/all_gather | solution.py:188
  104.7 10.6 %collective-permute-start.2 = (bf16[128,1152]{1,0:T(8,128)(2,1)S(1)}, bf16[128,1152]{1,0:T(8,128)(2,1)S(1)}, u32[]{:S(2)}, u32[]{:S(2)}) collective-permute-start(bf16[128,1152]{1,0:T(8,128)(2,1)S(1)} %bitcast_convert_fusion), channel_id=1, source_target_pairs={{16,0},{17,1},{18,2},{19,3},{20,4},{21,5},{22,6},{23,7},{24,8},{25... | collective-permute-start | bytes 884744 | tf_op jit(solution)/shard_map/ppermute | solution.py:17
  115.3 80.5 %copy-start.34 = (bf16[128,1152]{1,0:T(8,128)(2,1)}, bf16[128,1152]{1,0:T(8,128)(2,1)S(1)}, u32[]{:S(2)}) copy-start(bf16[128,1152]{1,0:T(8,128)(2,1)S(1)} %collective-permute-done.2) | copy-start | bytes 884740
  118.8 176.5 %all-gather.8.cloned.1.call-start = ((), (), s32[]{:S(2)}) async-start(), calls=%async_computation.6 | async-start | bytes 5013504 | tf_op jit(solution)/shard_map/all_gather | solution.py:134
  185.4 8.1 %collective-permute-start = (bf16[128,1152]{1,0:T(8,128)(2,1)S(1)}, bf16[128,1152]{1,0:T(8,128)(2,1)S(1)}, u32[]{:S(2)}, u32[]{:S(2)}) collective-permute-start(bf16[128,1152]{1,0:T(8,128)(2,1)S(1)} %fusion.38), channel_id=1, source_target_pairs={{0,16},{1,17},{2,18},{3,19},{4,20},{5,21},{6,22},{7,23},{8,24},{9,... | collective-permute-start | bytes 884744 | tf_op jit(solution)/shard_map/ppermute | solution.py:17
  194.9 104.6 %copy-start.32 = (f32[128]{0:T(128)}, f32[128]{0:T(128)S(1)}, u32[]{:S(2)}) copy-start(f32[128]{0:T(128)S(1)} %multiply_reduce_fusion.5) | copy-start | bytes 1540
  195.9 210.2 %reduce-scatter.7.cloned.1.call-start = ((), (), s32[]{:S(2)}) async-start(), calls=%async_computation.7 | async-start | bytes 5013504 | tf_op jit(solution)/shard_map/reduce_scatter | solution.py:145
  299.5 17.2 %copy-start.8 = (f32[2048,1,3,72]{0,3,2,1:T(8,128)}, f32[2048,1,3,72]{0,3,2,1:T(8,128)S(1)}, u32[]{:S(2)}) copy-start(f32[2048,1,3,72]{0,3,2,1:T(8,128)S(1)} %fusion.27) | copy-start | bytes 5308420
  327.9 158.9 %reduce-scatter.9.cloned.1.call-start = ((), (), s32[]{:S(2)}) async-start(), calls=%async_computation.9 | async-start | bytes 5013504 | tf_op jit(solution)/shard_map/reduce_scatter | solution.py:213
  339.6 19.9 %slice-start.4 = ((s8[16777216]{0:T(1024)(128)(4,1)}), s8[4194304]{0:T(1024)(128)(4,1)S(1)}, s32[]{:S(2)}) async-start(s8[16777216]{0:T(1024)(128)(4,1)} %bitcast.199), calls=%async_computation.17 | async-start | bytes 8388608
  339.6 19.9 %slice-start.5 = ((s8[16777216]{0:T(1024)(128)(4,1)}), s8[4194304]{0:T(1024)(128)(4,1)S(1)}, s32[]{:S(2)}) async-start(s8[16777216]{0:T(1024)(128)(4,1)} %bitcast.199), calls=%async_computation.18 | async-start | bytes 8388608
  339.6 19.9 %slice-start.6 = ((s8[16777216]{0:T(1024)(128)(4,1)}), s8[4194304]{0:T(1024)(128)(4,1)S(1)}, s32[]{:S(2)}) async-start(s8[16777216]{0:T(1024)(128)(4,1)} %bitcast.199), calls=%async_computation.19 | async-start | bytes 8388608
  353.0 4.3 copy-start.16
  353.1 4.3 copy-start.18
  353.1 4.3 copy-start.28
  353.1 6.4 slice-start.7
  363.2 124.8 %copy-start.33 = (f32[128]{0:T(128)S(1)}, f32[128]{0:T(128)}, u32[]{:S(2)}) copy-start(f32[128]{0:T(128)} %copy-done.32) | copy-start | bytes 1540
  367.1 189.5 %all-gather.12.cloned.1.call-start = ((), (), s32[]{:S(2)}) async-start(), calls=%async_computation.10 | async-start | bytes 5013504 | tf_op jit(solution)/shard_map/all_gather | solution.py:188
  409.3 78.8 %collective-permute-start.1 = (bf16[128,1152]{1,0:T(8,128)(2,1)}, bf16[128,1152]{1,0:T(8,128)(2,1)S(1)}, u32[]{:S(2)}, u32[]{:S(2)}) collective-permute-start(bf16[128,1152]{1,0:T(8,128)(2,1)} %fusion.41), channel_id=1, source_target_pairs={{0,16},{1,17},{2,18},{3,19},{4,20},{5,21},{6,22},{7,23},{8,24},{9,... | collective-permute-start | bytes 884744 | tf_op jit(solution)/shard_map/ppermute | solution.py:17
  490.4 9.1 %collective-permute-start.3 = (bf16[128,1152]{1,0:T(8,128)(2,1)S(1)}, bf16[128,1152]{1,0:T(8,128)(2,1)S(1)}, u32[]{:S(2)}, u32[]{:S(2)}) collective-permute-start(bf16[128,1152]{1,0:T(8,128)(2,1)S(1)} %fusion.151), channel_id=1, source_target_pairs={{16,0},{17,1},{18,2},{19,3},{20,4},{21,5},{22,6},{23,7},{24,8},{25... | collective-permute-start | bytes 884744 | tf_op jit(solution)/shard_map/ppermute | solution.py:17
  503.2 57.6 %copy-start.20 = (f32[2048]{0:T(1024)S(1)}, f32[2048]{0:T(1024)}, u32[]{:S(2)}) copy-start(f32[2048]{0:T(1024)} %copy-done.19) | copy-start | bytes 24580
  503.2 57.6 %copy-start.22 = (f32[2048]{0:T(1024)S(1)}, f32[2048]{0:T(1024)}, u32[]{:S(2)}) copy-start(f32[2048]{0:T(1024)} %copy-done.21) | copy-start | bytes 24580
  503.2 144.9 %all-reduce.3.cloned.1.call-start = ((), (), s32[]{:S(2)}) async-start(), calls=%async_computation.12 | async-start | bytes 2654208 | tf_op jit(solution)/shard_map/psum | solution.py:228
  556.6 12.0 %slice-start = ((s8[16777216]{0:T(1024)(128)(4,1)}), s8[4194304]{0:T(1024)(128)(4,1)S(1)}, s32[]{:S(2)}) async-start(s8[16777216]{0:T(1024)(128)(4,1)} %bitcast.197), calls=%async_computation.13 | async-start | bytes 8388608
  560.8 7.8 %slice-start.1 = ((s8[16777216]{0:T(1024)(128)(4,1)}), s8[4194304]{0:T(1024)(128)(4,1)S(1)}, s32[]{:S(2)}) async-start(s8[16777216]{0:T(1024)(128)(4,1)} %bitcast.197), calls=%async_computation.14 | async-start | bytes 8388608
  560.8 8.2 %slice-start.2 = ((s8[16777216]{0:T(1024)(128)(4,1)}), s8[4194304]{0:T(1024)(128)(4,1)S(1)}, s32[]{:S(2)}) async-start(s8[16777216]{0:T(1024)(128)(4,1)} %bitcast.197), calls=%async_computation.15 | async-start | bytes 8388608
  560.8 9.4 %slice-start.3 = ((s8[16777216]{0:T(1024)(128)(4,1)}), s8[4194304]{0:T(1024)(128)(4,1)S(1)}, s32[]{:S(2)}) async-start(s8[16777216]{0:T(1024)(128)(4,1)} %bitcast.197), calls=%async_computation.16 | async-start | bytes 8388608
  579.1 8.5 %copy-start.3 = (bf16[2048,2,72]{0,2,1:T(8,128)(2,1)S(1)}, bf16[2048,2,72]{0,2,1:T(8,128)(2,1)}, u32[]{:S(2)}) copy-start(bf16[2048,2,72]{0,2,1:T(8,128)(2,1)} %copy-done.2) | copy-start | bytes 1769476
  587.6 4.2 copy-start.5
  590.3 7.9 %slice-start.8 = ((s8[4718592]{0:T(1024)(128)(4,1)}), s8[4194304]{0:T(1024)(128)(4,1)S(1)}, s32[]{:S(2)}) async-start(s8[4718592]{0:T(1024)(128)(4,1)} %bitcast.211), calls=%async_computation.21 | async-start | bytes 8388608
  591.9 6.3 slice-start.9
  595.2 5.8 copy-start.6
  600.6 129.4 %copy-start.1 = (bf16[1,1,128,1152]{3,2,1,0:T(8,128)(2,1)S(1)}, bf16[1,1,128,1152]{3,2,1,0:T(8,128)(2,1)}, u32[]{:S(2)}) copy-start(bf16[1,1,128,1152]{3,2,1,0:T(8,128)(2,1)} %param.8) | copy-start | bytes 884740
  600.6 129.4 %copy-start.14 = (f32[1152]{0:T(1024)S(1)}, f32[1152]{0:T(1024)}, u32[]{:S(2)}) copy-start(f32[1152]{0:T(1024)} %copy-done.13) | copy-start | bytes 13828
  600.7 129.4 %copy-start.24 = (f32[128]{0:T(128)S(1)}, f32[128]{0:T(128)}, u32[]{:S(2)}) copy-start(f32[128]{0:T(128)} %copy-done.23) | copy-start | bytes 1540
  600.7 129.4 %reduce-scatter.11.cloned.1.call-start = ((), (), s32[]{:S(2)}) async-start(), calls=%async_computation.11 | async-start | bytes 5013504 | tf_op jit(solution)/shard_map/reduce_scatter | solution.py:213
  601.0 130.3 %copy-start.31 = (f32[128]{0:T(128)S(1)}, f32[128]{0:T(128)}, u32[]{:S(2)}) copy-start(f32[128]{0:T(128)} %copy-done.30) | copy-start | bytes 1540
  601.0 130.3 %copy-start.26 = (f32[128]{0:T(128)S(1)}, f32[128]{0:T(128)}, u32[]{:S(2)}) copy-start(f32[128]{0:T(128)} %copy-done.25) | copy-start | bytes 1540
  601.0 131.6 %copy-start.10 = (f32[128,1152]{1,0:T(8,128)S(1)}, f32[128,1152]{1,0:T(8,128)}, u32[]{:S(2)}) copy-start(f32[128,1152]{1,0:T(8,128)} %get-tuple-element.156) | copy-start | bytes 1769476
  (10 other events, 15.1 us)
Sparse Core Ops, SparseCore 0:
  13.6 56.5 all-gather.5
  104.7 78.2 reduce-scatter.4
  185.7 53.3 all-gather.9
  241.6 53.6 all-gather.7
  328.1 78.0 reduce-scatter.6
  409.3 77.5 reduce-scatter.8
  503.3 53.2 all-gather.11
  600.8 47.2 all-reduce.2
  651.5 78.5 reduce-scatter.10
where the time goes:
time: 752 us; the launch traced here: 742 us
  waiting for transfers between devices  488 us (65%)
  matrix products  128 us (17%)
  other arithmetic  67.4 us (9%)
  blocking collectives  22.2 us (3%)
  between operations  16.8 us (2%)
  starting transfers between devices  10.7 us (1%)
  local copies, waits for them, and re-layouts  7.72 us (1%)
    reduce_scatter x2, waiting for transfers between devices, local(): lax.psum_scatter(jnp.dot(d_raw, qkv_rows[block_index], preferred_element_...  151 us
    reduce_scatter x2, waiting for transfers between devices, local(): lax.psum_scatter(jnp.dot(mixed_heads, out_rows[block_index], preferred_el...  102 us
    all_gather x2, waiting for transfers between devices, local(): d_full = lax.all_gather(d_attn, 'seq', axis=0, tiled=True)  87.5 us
    all_gather x2, waiting for transfers between devices, local(): gathered = lax.all_gather(normed, 'seq', axis=0, tiled=True)  84 us
    psum x1, waiting for transfers between devices, local(): lax.psum(jnp.stack(qkv_grads).astype(jnp.bfloat16), 'dp')  43.3 us
    all_gather x1, blocking collectives, local(): lax.all_gather(positions, 'seq', axis=0, tiled=True)  22.2 us
    convert_element_type x2, other arithmetic, back_head(): grad_scores = (probs * centred / math.sqrt(head_size)).astype(jnp.bfloat16)  21.9 us
    dot_general x2, matrix products, back_head(): lax.dot_general(grad_heads, values_in, (((1,), (1,)), ((), ())), preferre...  20.4 us
  transfers between devices with their start and end apart: 13, of which 12 were waited for; matrix products, arithmetic and copies ran while one was open for 10% of the time, Pallas kernels for 0%

commit v1 on v0

v1 whole, which is shorter than its diff:
```python
import math

import jax
import jax.numpy as jnp
from jax import lax
from jax.experimental import pallas as pl
from jax.experimental.pallas import tpu as pltpu
from jax.sharding import PartitionSpec as P

GRID_W = 128
HS = 72
HP = 80
HALF = 40
QB = 256
TB = 128
SCALE = 1.0 / math.sqrt(HS)
EXP_SCALE = math.log2(math.e) / math.sqrt(HS)

norm_eps = 1e-06
bf = jnp.bfloat16
f32 = jnp.float32


def nn(a, b):
    return lax.dot_general(a, b, (((1,), (0,)), ((), ())), preferred_element_type=f32)


def nt(a, b):
    return lax.dot_general(a, b, (((1,), (1,)), ((), ())), preferred_element_type=f32)


def tn(a, b):
    return lax.dot_general(a, b, (((0,), (0,)), ((), ())), preferred_element_type=f32)


def flat(ref, to_ref):
    for j in range(ref.shape[0]):
        to_ref[:, j * TB : (j + 1) * TB] = ref[j]


def put(ref, i, value):
    for j in range(QB // TB):
        ref[i * (QB // TB) + j] = value[:, j * TB : (j + 1) * TB]


def turn_back(x, c, s):
    a, b = x[:HALF], x[HALF:]
    return jnp.concatenate([a * c + b * s, b * c - a * s], axis=0)


def with_ones(v):
    rows = lax.broadcasted_iota(jnp.int32, v.shape, 0)
    return jnp.where(rows == HS, 1.0, v.astype(f32)).astype(bf)


def fwd_kernel(x_ref, o_ref, l_ref, kt_ref, vo_ref):
    i = pl.program_id(0)

    @pl.when(i == 0)
    def _():
        kt_ref[...] = x_ref[HP : 2 * HP].astype(f32).T.astype(bf)
        vo_ref[...] = with_ones(x_ref[2 * HP :])

    s = nn(kt_ref[...], x_ref[:HP, pl.ds(pl.multiple_of(i * QB, QB), QB)])
    m = jnp.max(s, axis=0, keepdims=True)
    e = jnp.exp2((s - m) * EXP_SCALE).astype(bf)
    o = nn(vo_ref[...], e)
    total = o[HS : HS + 1]
    rows = lax.broadcasted_iota(jnp.int32, o.shape, 0)
    put(o_ref, i, jnp.where(rows < HS, o * (1.0 / total), 0.0).astype(bf))
    l_ref[...] = m * EXP_SCALE + jnp.log2(total)


def attn_fwd(x):
    n = x.shape[1]
    return pl.pallas_call(
        fwd_kernel,
        grid=(n // QB,),
        in_specs=[pl.BlockSpec((3 * HP, n), lambda i: (0, 0))],
        out_specs=[
            pl.BlockSpec((n // TB, HP, TB), lambda i: (0, 0, 0)),
            pl.BlockSpec((1, QB), lambda i: (0, i)),
        ],
        out_shape=[jax.ShapeDtypeStruct((n // TB, HP, TB), bf), jax.ShapeDtypeStruct((1, n), f32)],
        scratch_shapes=[pltpu.VMEM((n, HP), bf), pltpu.VMEM((HP, n), bf)],
        compiler_params=pltpu.CompilerParams(vmem_limit_bytes=40 * 2**20),
        cost_estimate=pl.CostEstimate(flops=4 * n * n * 256, bytes_accessed=2 * 4 * HP * n, transcendentals=n * n),
        name="attn_fwd",
    )(x)


def prep(x_ref, kt_ref, vt_ref, dk_ref, dv_ref):
    kt_ref[...] = x_ref[HP : 2 * HP].astype(f32).T.astype(bf)
    vt_ref[...] = x_ref[2 * HP :].astype(f32).T.astype(bf)
    dk_ref[...] = jnp.zeros_like(dk_ref)
    dv_ref[...] = jnp.zeros_like(dv_ref)


def finish(i, dq, c_ref, s_ref, d_ref, db_ref, dk_ref, dv_ref):
    at = pl.ds(pl.multiple_of(i * QB, QB), QB)
    d_ref[:HP, at] = turn_back(dq * SCALE, c_ref[:, at], s_ref[:, at]).astype(bf)

    @pl.when(i == pl.num_programs(0) - 1)
    def _():
        d_ref[HP : 2 * HP, :] = turn_back(dk_ref[...].T * SCALE, c_ref[...], s_ref[...]).astype(bf)
        d_ref[2 * HP :, :] = dv_ref[...].T.astype(bf)
        for j in range(db_ref.shape[0]):
            db_ref[j] = d_ref[:, j * TB : (j + 1) * TB]


def bwd_kernel(x_ref, g_ref, o_ref, l_ref, c_ref, s_ref, d_ref, db_ref, kt_ref, vt_ref, dk_ref, dv_ref, gx_ref, ox_ref):
    i = pl.program_id(0)

    @pl.when(i == 0)
    def _():
        prep(x_ref, kt_ref, vt_ref, dk_ref, dv_ref)
        flat(g_ref, gx_ref)
        flat(o_ref, ox_ref)

    at = pl.ds(pl.multiple_of(i * QB, QB), QB)
    q = x_ref[:HP, at]
    g = gx_ref[:, at]
    p = jnp.exp2(nn(kt_ref[...], q) * EXP_SCALE - l_ref[...])
    delta = jnp.sum(g.astype(f32) * ox_ref[:, at].astype(f32), axis=0, keepdims=True)
    ds = (p * (nn(vt_ref[...], g) - delta)).astype(bf)
    dv_ref[...] += nt(p.astype(bf), g)
    dk_ref[...] += nt(ds, q)
    finish(i, nn(x_ref[HP : 2 * HP], ds), c_ref, s_ref, d_ref, db_ref, dk_ref, dv_ref)


def both_kernel(xb_ref, gb_ref, c_ref, s_ref, o_ref, d_ref, db_ref, kt_ref, vt_ref, dk_ref, dv_ref, x_ref, g_ref, vo_ref):
    i = pl.program_id(0)

    @pl.when(i == 0)
    def _():
        flat(xb_ref, x_ref)
        flat(gb_ref, g_ref)
        prep(x_ref, kt_ref, vt_ref, dk_ref, dv_ref)
        vo_ref[...] = with_ones(x_ref[2 * HP :])

    at = pl.ds(pl.multiple_of(i * QB, QB), QB)
    q = x_ref[:HP, at]
    s = nn(kt_ref[...], q)
    m = jnp.max(s, axis=0, keepdims=True)
    e = jnp.exp2((s - m) * EXP_SCALE)
    eb = e.astype(bf)
    o = nn(vo_ref[...], eb)
    inv = 1.0 / o[HS : HS + 1]
    rows = lax.broadcasted_iota(jnp.int32, o.shape, 0)
    o = jnp.where(rows < HS, o * inv, 0.0)
    put(o_ref, i, o.astype(bf))
    g = g_ref[:, at].astype(f32) * inv
    delta = jnp.sum(g * o, axis=0, keepdims=True)
    g = g.astype(bf)
    ds = (e * (nn(vt_ref[...], g) - delta)).astype(bf)
    dv_ref[...] += nt(eb, g)
    dk_ref[...] += nt(ds, q)
    finish(i, nn(x_ref[HP : 2 * HP], ds), c_ref, s_ref, d_ref, db_ref, dk_ref, dv_ref)


def whole(x):
    zeros = (0,) * x.ndim
    return pl.BlockSpec(x.shape, lambda i: zeros)


def back_call(kernel, ins, in_specs, n, extra_out, extra_scratch, name):
    d_shapes = [jax.ShapeDtypeStruct((3 * HP, n), bf), jax.ShapeDtypeStruct((n // TB, 3 * HP, TB), bf)]
    out_shape = extra_out + d_shapes
    scratch = [pltpu.VMEM((n, HP), bf), pltpu.VMEM((n, HP), bf), pltpu.VMEM((n, HP), f32), pltpu.VMEM((n, HP), f32)]
    return pl.pallas_call(
        kernel,
        grid=(n // QB,),
        in_specs=in_specs,
        out_specs=[whole(x) for x in out_shape],
        out_shape=out_shape,
        scratch_shapes=scratch + extra_scratch,
        compiler_params=pltpu.CompilerParams(vmem_limit_bytes=48 * 2**20),
        cost_estimate=pl.CostEstimate(flops=10 * n * n * 256, bytes_accessed=2 * 12 * HP * n, transcendentals=n * n),
        name=name,
    )(*ins)


def attn_bwd(x, g, o, l, c, s):
    n = x.shape[1]
    specs = [whole(x), whole(g), whole(o), pl.BlockSpec((1, QB), lambda i: (0, i)), whole(c), whole(s)]
    extra = [pltpu.VMEM((HP, n), bf), pltpu.VMEM((HP, n), bf)]
    return back_call(bwd_kernel, (x, g, o, l, c, s), specs, n, [], extra, "attn_bwd")


def attn_both(x, g, c, s):
    n = x.shape[0] * TB
    extra = [pltpu.VMEM((3 * HP, n), bf), pltpu.VMEM((HP, n), bf), pltpu.VMEM((HP, n), bf)]
    out = [jax.ShapeDtypeStruct((n // TB, HP, TB), bf)]
    return back_call(both_kernel, (x, g, c, s), [whole(x), whole(g), whole(c), whole(s)], n, out, extra, "attn_both")


def swap(value, axis, bit):
    count = lax.axis_size(axis)
    return lax.ppermute(value, axis, [(i, i ^ bit) for i in range(count)])


def shifted(value, axis, by):
    count = lax.axis_size(axis)
    pairs = [(i, i + by) for i in range(count) if 0 <= i + by < count]
    return lax.ppermute(value, axis, pairs)


def scatter_heads(value):
    return lax.all_to_all(value, "seq", split_axis=0, concat_axis=0, tiled=True)


def angle_tables(places):
    quarter = HS // 4
    freqs = jnp.exp(-math.log(10000.0) * jnp.arange(quarter, dtype=f32) / quarter)
    grid_rows = (places // GRID_W).astype(f32)
    grid_cols = (places % GRID_W).astype(f32)
    angles = jnp.concatenate(
        [
            freqs[:, None] * grid_rows[None, :],
            freqs[:, None] * grid_cols[None, :],
            jnp.zeros((HALF - 2 * quarter, places.shape[0]), f32),
        ],
        axis=0,
    )
    return jnp.cos(angles), jnp.sin(angles)


def pad_rows(x, count):
    return jnp.pad(x, ((0, count - x.shape[0]), (0, 0)))


def arrange(w):
    qt = HS // 4
    parts = []
    for part in (w[0], w[1]):
        parts += [pad_rows(jnp.concatenate([part[0:qt], part[2 * qt : 3 * qt]]), HALF)]
        parts += [pad_rows(jnp.concatenate([part[qt : 2 * qt], part[3 * qt :]]), HALF)]
    return jnp.concatenate(parts + [pad_rows(w[2], HP)], axis=0)


def disarrange(g):
    qt = HS // 4
    parts = []
    for at in (0, HP):
        a, b = g[at : at + HALF], g[at + HALF : at + HP]
        parts += [a[:qt], b[:qt], a[qt : 2 * qt], b[qt : 2 * qt]]
    return jnp.concatenate(parts + [g[2 * HP : 2 * HP + HS]], axis=0).reshape(3, HS, g.shape[1])


def rope(qa, qb, ka, kb, v, c, s):
    return jnp.concatenate([qa * c - qb * s, qa * s + qb * c, ka * c - kb * s, ka * s + kb * c, v], axis=-2).astype(bf)


def modulated_norm(hidden, shift_vec, scale_vec):
    centre = hidden - jnp.mean(hidden, axis=-1, keepdims=True)
    spread = jnp.mean(centre * centre, axis=-1, keepdims=True)
    return centre * lax.rsqrt(spread + norm_eps) * (1.0 + scale_vec) + shift_vec


def norm_back(hidden, scale_vec, grad):
    centre = hidden - jnp.mean(hidden, axis=-1, keepdims=True)
    inv = lax.rsqrt(jnp.mean(centre * centre, axis=-1, keepdims=True) + norm_eps)
    unit = centre * inv
    grad = grad * (1.0 + scale_vec)
    return inv * (grad - jnp.mean(grad, axis=-1, keepdims=True) - unit * jnp.mean(grad * unit, axis=-1, keepdims=True))


def dp_sum(value):
    own = value.astype(bf)
    both = (own.astype(f32) + swap(own, "dp", 1).astype(f32)).astype(bf)
    return both.astype(f32) + swap(both, "dp", 2).astype(f32)


def local(streams, modulation, w_qkv, w_out, w_zero, pairing, positions, cotangent):
    on_main = lax.axis_index("section") == 1
    core = lax.axis_index("dp") % 2
    first = core == 0
    mods = modulation[0]
    pair_row = pairing[0]
    width = streams.shape[-1]
    seqs = lax.axis_size("seq")
    qkv_w = [arrange(w_qkv[0, k, 0]) for k in range(2)]
    out_w = [pad_rows(w_out[0, k, 0], HP) for k in range(2)]

    def own_half(w):
        rows = w.shape[0] // 2
        return lax.dynamic_slice_in_dim(w, core * rows, rows, axis=0)

    def gather(x):
        return lax.all_gather(x, "seq", axis=0, tiled=False)

    def rows_of(w):
        return w.reshape(-1, width)

    def halves_of(x):
        rows = x.shape[1] // 2
        low, high = x[:, :rows], x[:, rows:]
        mine = jnp.where(first, low, high)
        theirs = jnp.where(first, high, low)
        return mine.reshape(-1, x.shape[2]), theirs.reshape(-1, x.shape[2])

    def to_heads(w_pair, x):
        mine, theirs = [nt(rows_of(w), x).reshape(seqs, -1, x.shape[0]) for w in w_pair]
        return jnp.where(first, mine, theirs), jnp.where(first, theirs, mine)

    def from_heads(w_pair, x):
        mine, theirs = halves_of(x)
        return tn(mine, rows_of(w_pair[0])) + tn(theirs, rows_of(w_pair[1]))

    hidden0 = streams[0, 0].astype(f32)
    normed0 = modulated_norm(hidden0, mods[0, 0], mods[0, 1]).astype(bf)
    normed0_all = gather(normed0).reshape(-1, width)
    piece_1 = gather(jnp.concatenate([own_half(out_w[0]), own_half(out_w[1]), own_half(qkv_w[1])], axis=0))
    cuts = (HP // 2, HP, HP + 3 * HP // 2)

    def with_other(x):
        return (x, swap(x, "dp", 1))

    out_full0 = with_other(piece_1[:, : cuts[0]])
    out_full1 = with_other(piece_1[:, cuts[0] : cuts[1]])
    qkv_full1 = with_other(piece_1[:, cuts[1] :])

    everywhere = scatter_heads(jnp.broadcast_to(positions[None, None, :], (seqs, 1, positions.shape[0])))
    cos_all, sin_all = angle_tables(everywhere.reshape(-1))
    cos_own, sin_own = angle_tables(positions)

    cot = cotangent[0]
    through = nt(cot, w_zero[1])
    grad2 = jnp.where(on_main, cot.astype(f32), jnp.where(pair_row[1] == 1, through, 0.0))
    d_attn1 = (mods[1, 2] * grad2).astype(bf)
    low, high = to_heads(out_full1, d_attn1)
    d_mixed1 = scatter_heads(jnp.concatenate([low, high], axis=1).astype(bf))

    raw = nt(qkv_w[0], normed0_all)
    qkv0 = rope(raw[:HALF], raw[HALF:HP], raw[HP : HP + HALF], raw[HP + HALF : 2 * HP], raw[2 * HP :], cos_all, sin_all)
    mixed0, log_sums0 = attn_fwd(qkv0)
    attn0 = from_heads(out_full0, scatter_heads(mixed0))
    hidden1 = hidden0 + mods[0, 2] * attn0
    zero0 = shifted(nn(hidden1.astype(bf), w_zero[0]).astype(bf), "section", 1).astype(f32)
    hidden1 = hidden1 + jnp.where(pair_row[0] == 0, zero0, 0.0)

    normed1 = modulated_norm(hidden1, mods[1, 0], mods[1, 1]).astype(bf)
    low, high = to_heads(qkv_full1, normed1)
    qkv1 = rope(low[:, :HALF], low[:, HALF:HP], low[:, HP:], high[:, :HALF], high[:, HALF:], cos_own, sin_own)
    mixed1, d_raw1, d_raw1_blocks = attn_both(scatter_heads(qkv1), d_mixed1, cos_all, sin_all)
    d_normed1 = from_heads(qkv_full1, scatter_heads(d_raw1_blocks))
    grad1 = grad2 + norm_back(hidden1, mods[1, 1], d_normed1)

    attn1 = from_heads(out_full1, scatter_heads(mixed1))
    hidden2 = hidden1 + mods[1, 2] * attn1
    zero1 = shifted(nn(hidden2.astype(bf), w_zero[1]).astype(bf), "section", 1).astype(f32)
    hidden2 = hidden2 + jnp.where(pair_row[0] == 1, zero0, 0.0) + jnp.where(pair_row[1] == 1, zero1, 0.0)
    final_out = hidden2.astype(bf)[None, None]

    sent = shifted(grad1.astype(bf), "section", -1)
    picked = jnp.where(pair_row[0] == 0, sent, cot)
    picked = jnp.where(on_main, jnp.zeros_like(picked), picked)
    grad1 = grad1 + nt(picked, w_zero[0])
    d_attn0 = (mods[0, 2] * grad1).astype(bf)
    low, high = to_heads(out_full0, d_attn0)
    d_mixed0 = scatter_heads(jnp.concatenate([low, high], axis=1).astype(bf))
    d_raw0, d_raw0_blocks = attn_bwd(qkv0, d_mixed0, mixed0, log_sums0, cos_all, sin_all)
    later = gather(jnp.concatenate([d_attn1, normed1, own_half(qkv_w[0])], axis=0))
    qkv_full0 = with_other(later[:, 2 * TB :])
    d_normed0 = from_heads(qkv_full0, scatter_heads(d_raw0_blocks))
    grad0 = grad1 + norm_back(hidden0, mods[0, 1], d_normed0)

    d_attn1_all = later[:, :TB].reshape(-1, width)
    normed1_all = later[:, TB : 2 * TB].reshape(-1, width)
    d_attn0_all = gather(d_attn0).reshape(-1, width)

    def tokens_last(x):
        return jnp.moveaxis(x, 0, 1).reshape(x.shape[1], -1)

    block_1 = dp_sum(jnp.concatenate([nn(d_raw1, normed1_all), nn(tokens_last(mixed1), d_attn1_all)], axis=0))
    qkv_grad0 = dp_sum(nn(d_raw0, normed0_all))
    out_grad0 = dp_sum(nn(tokens_last(mixed0), d_attn0_all))
    grad_qkv = jnp.stack([disarrange(qkv_grad0), disarrange(block_1[: 3 * HP])])[None, :, None]
    grad_out = jnp.stack([out_grad0[:HS], block_1[3 * HP : 3 * HP + HS]])[None, :, None]
    return (final_out, grad0[None, None], grad_qkv, grad_out)


def solution(mesh):
    in_specs = (
        P("section", "dp", "seq", None),
        P("section", None, None, None),
        P("section", None, "seq", None, None, None),
        P("section", None, "seq", None, None),
        P(),
        P("dp", None),
        P("seq"),
        P("dp", "seq", None),
    )
    out_specs = (
        P("section", "dp", "seq", None),
        P("section", "dp", "seq", None),
        P("section", None, "seq", None, None, None),
        P("section", None, "seq", None, None),
    )
    return jax.shard_map(local, mesh=mesh, in_specs=in_specs, out_specs=out_specs, check_vma=False)
```

time: 752 us -> 510 us (0.68); the launches traced: 742 us -> 508 us
  waiting for transfers between devices: 488 us -> 240 us
  matrix products: 128 us -> 63.3 us
  Pallas kernels: 0 us -> 46.3 us
  other arithmetic: 67.4 us -> 24.6 us
  starting transfers between devices: 10.7 us -> 43.1 us
  local copies, waits for them, and re-layouts: 7.72 us -> 34 us
  blocking collectives: 22.2 us -> 40 us
    reduce_scatter x4 -> x0, waiting for transfers between devices: 254 us -> none  [the longest x2 151 us: local(): lax.psum_scatter(jnp.dot(d_raw, qkv_rows[block_index], preferred_element_...]
    dot_general x28 -> x23, matrix products: 128 us -> 63.3 us  [the longest x9 25 us: nt(): lax.dot_general(a, b, (((1,), (1,)), ((), ())), preferred_element_type=f32)]
    pallas_call x0 -> x3, Pallas kernels: none -> 46.3 us  [the longest x2 35.6 us: back_call(): pl.pallas_call(kernel, grid=(n // QB,), in_specs=in_specs, out_specs=[who...]
    psum x1 -> x0, waiting for transfers between devices: 43.3 us -> none  [local(): lax.psum(jnp.stack(qkv_grads).astype(jnp.bfloat16), 'dp')]
    all_to_all x0 -> x2, blocking collectives: none -> 40 us  [scatter_heads(): return lax.all_to_all(value, 'seq', split_axis=0, concat_axis=0, tiled=True)]
    all_to_all x0 -> x6, starting transfers between devices: none -> 28.6 us  [scatter_heads(): return lax.all_to_all(value, 'seq', split_axis=0, concat_axis=0, tiled=True)]
    ppermute x0 -> x10, waiting for transfers between devices: none -> 25.1 us  [swap(): return lax.ppermute(value, axis, [(i, i ^ bit) for i in range(count)])]
    all_to_all x0 -> x6, waiting for transfers between devices: none -> 23.1 us  [scatter_heads(): return lax.all_to_all(value, 'seq', split_axis=0, concat_axis=0, tiled=True)]
  transfers between devices with their start and end apart: 13 -> 23, of which waited for: 12 -> 12; matrix products, arithmetic and copies ran while one was open for 10% -> 19% of each run, Pallas kernels for 0% -> 5%
where the time goes in v1:
time: 510 us; the launch traced here: 508 us
  waiting for transfers between devices  240 us (47%)
  matrix products  63.3 us (12%)
  Pallas kernels  46.3 us (9%)
  starting transfers between devices  43.1 us (8%)
  blocking collectives  40 us (8%)
  local copies, waits for them, and re-layouts  34 us (7%)
  other arithmetic  24.6 us (5%)
  between operations  16.8 us (3%)
    all_gather x4, waiting for transfers between devices, gather(): return lax.all_gather(x, 'seq', axis=0, tiled=False)  180 us
    all_to_all x2, blocking collectives, scatter_heads(): return lax.all_to_all(value, 'seq', split_axis=0, concat_axis=0, tiled=True)  40 us
    pallas_call x2, Pallas kernels, back_call(): pl.pallas_call(kernel, grid=(n // QB,), in_specs=in_specs, out_specs=[who...  35.6 us
    all_to_all x6, starting transfers between devices, scatter_heads(): return lax.all_to_all(value, 'seq', split_axis=0, concat_axis=0, tiled=True)  28.6 us
    ppermute x10, waiting for transfers between devices, swap(): return lax.ppermute(value, axis, [(i, i ^ bit) for i in range(count)])  25.1 us
    dot_general x9, matrix products, nt(): lax.dot_general(a, b, (((1,), (1,)), ((), ())), preferred_element_type=f32)  25 us
    all_to_all x6, waiting for transfers between devices, scatter_heads(): return lax.all_to_all(value, 'seq', split_axis=0, concat_axis=0, tiled=True)  23.1 us
    dot_general x8, matrix products, tn(): lax.dot_general(a, b, (((0,), (0,)), ((), ())), preferred_element_type=f32)  21.3 us
  transfers between devices with their start and end apart: 23, of which 12 were waited for; matrix products, arithmetic and copies ran while one was open for 19% of the time, Pallas kernels for 5%

profile of v1, /device:TPU:0, one launch (start us, length us, event | category | flops | bytes accessed | tf_op | source)
XLA Modules:
  0.0 507.8 jit_solution(12601597042557191318)
XLA Ops:
  17.3 8.1 %all-to-all-start = ((s32[16,1,128]{2,1,0:T(1,128)}), s32[16,1,128]{2,1,0:T(1,128)S(1)}, u32[]{:S(2)}, u32[]{:S(2)}) async-start(s32[16,1,128]{2,1,0:T(1,128)} %broadcast_in_dim.23), calls=%async_computation | async-start | bytes 16384 | tf_op jit(solution)/shard_map/all_to_all | solution.py:209
  28.6 4.4 all-to-all-done
  33.1 36.7 %all-gather.8.cloned.1.call-done = bf16[16,128,1152]{2,1,0:T(8,128)(2,1)} async-done(((bf16[1,128,1152]{2,1,0:T(8,128)(2,1)}), bf16[16,128,1152]{2,1,0:T(8,128)(2,1)}) %all-gather.8.cloned.1.call-update) | async-done | bytes 4718608 | tf_op jit(solution)/shard_map/all_gather | solution.py:290
  69.8 3.9 fusion.194
  75.4 63.2 %all-gather.10.cloned.1.call-done = bf16[3200,1152]{1,0:T(8,128)(2,1)} async-done(((bf16[200,1152]{1,0:T(8,128)(2,1)}), bf16[3200,1152]{1,0:T(8,128)(2,1)}) %all-gather.10.cloned.1.call-update) | async-done | bytes 7372816 | tf_op jit(solution)/shard_map/all_gather | solution.py:290
  138.6 3.2 fusion.190
  141.8 4.7 slice.449
  148.2 10.7 %attn_fwd.1 = (bf16[16,80,128]{2,1,0:T(8,128)(2,1)}, f32[1,2048]{1,0:T(1,128)S(1)}) custom-call(bf16[240,2048]{1,0:T(8,128)(2,1)S(1)} %fusion.82.x_ref), custom_call_target="tpu_custom_call" | custom-call | flops 4294967296 | bytes 1310720 | tf_op jit(solution)/shard_map/attn_fwd/pallas_call | solution.py:76
  158.9 5.3 %all-to-all-start.1 = ((bf16[16,80,128]{2,1,0:T(8,128)(2,1)}), bf16[16,80,128]{2,1,0:T(8,128)(2,1)}, u32[]{:S(2)}, u32[]{:S(2)}) async-start(bf16[16,80,128]{2,1,0:T(8,128)(2,1)} %get-tuple-element.11.o_ref), calls=%async_computation.1 | async-start | bytes 655360 | tf_op jit(solution)/shard_map/all_to_all | solution.py:209
  164.3 3.6 multiply_convert_fusion.1
  167.9 6.5 %all-to-all-done.1 = bf16[16,80,128]{2,1,0:T(8,128)(2,1)} async-done(((bf16[16,80,128]{2,1,0:T(8,128)(2,1)}), bf16[16,80,128]{2,1,0:T(8,128)(2,1)}, u32[]{:S(2)}, u32[]{:S(2)}) %all-to-all-start.1) | async-done | bytes 327712 | tf_op jit(solution)/shard_map/all_to_all | solution.py:209
  176.4 2.0 fusion.93
  178.4 2.0 fusion.28
  180.5 2.4 fusion.29
  182.9 3.5 collective-permute-start.1
  189.2 3.5 all-to-all-start.3
  193.6 3.9 fusion.100
  197.5 3.7 broadcast_select_fusion
  205.0 22.8 %all_to_all.40.xb_ref = bf16[16,240,128]{2,1,0:T(8,128)(2,1)S(1)} all-to-all(bf16[16,240,128]{2,1,0:T(8,128)(2,1)} %fusion.83), channel_id=1, replica_groups=mesh['dp'=4,'section'=2,'seq'=16] {'seq'}, dimensions={0} | all-to-all | bytes 1966080 | tf_op jit(solution)/shard_map/all_to_all | solution.py:209
  227.8 21.2 %attn_both.1 = (bf16[16,80,128]{2,1,0:T(8,128)(2,1)}, bf16[240,2048]{1,0:T(8,128)(2,1)S(1)}, bf16[16,240,128]{2,1,0:T(8,128)(2,1)S(1)}) custom-call(bf16[16,240,128]{2,1,0:T(8,128)(2,1)S(1)} %all_to_all.40.xb_ref, bf16[16,80,128]{2,1,0:T(8,128)(2,1)S(1)} %all-to-all-done.3.gb_ref, f32[40,2048]{1,0:T(8,128)S(1)} %get-tuple-element.41.c_ref, ...), custom_call_target="tpu_custom_call" | custom-call | flops 10737418240 | bytes 3932160 | tf_op jit(solution)/shard_map/attn_both/pallas_call | solution.py:170
  249.0 17.2 %all_to_all.41 = bf16[16,240,128]{2,1,0:T(8,128)(2,1)S(1)} all-to-all(bf16[16,240,128]{2,1,0:T(8,128)(2,1)S(1)} %get-tuple-element.13), channel_id=1, replica_groups=mesh['dp'=4,'section'=2,'seq'=16] {'seq'}, dimensions={0} | all-to-all | bytes 1966080 | tf_op jit(solution)/shard_map/all_to_all | solution.py:209
  267.1 3.8 fusion.184
  272.6 7.3 %collective-permute-done.5 = bf16[128,1152]{1,0:T(8,128)(2,1)S(1)} collective-permute-done((bf16[128,1152]{1,0:T(8,128)(2,1)S(1)}, bf16[128,1152]{1,0:T(8,128)(2,1)S(1)}, u32[]{:S(2)}, u32[]{:S(2)}) %collective-permute-start.5) | collective-permute-done | bytes 294944 | tf_op jit(solution)/shard_map/ppermute | solution.py:205
  284.9 3.6 all-to-all-start.4
  288.4 2.1 fusion.89
  293.3 6.3 %all-to-all-done.4 = bf16[16,80,128]{2,1,0:T(8,128)(2,1)S(1)} async-done(((bf16[16,80,128]{2,1,0:T(8,128)(2,1)}), bf16[16,80,128]{2,1,0:T(8,128)(2,1)S(1)}, u32[]{:S(2)}, u32[]{:S(2)}) %all-to-all-start.4) | async-done | bytes 327712 | tf_op jit(solution)/shard_map/all_to_all | solution.py:209
  300.3 3.8 all-to-all-start.6
  304.1 2.8 convolution_bitcast_fusion.5
  306.9 6.0 %all-to-all-done.6.g_ref = bf16[16,80,128]{2,1,0:T(8,128)(2,1)S(1)} async-done(((bf16[16,80,128]{2,1,0:T(8,128)(2,1)}), bf16[16,80,128]{2,1,0:T(8,128)(2,1)S(1)}, u32[]{:S(2)}, u32[]{:S(2)}) %all-to-all-start.6) | async-done | bytes 327712 | tf_op jit(solution)/shard_map/all_to_all | solution.py:209
  312.9 14.3 %attn_bwd.1 = (bf16[240,2048]{1,0:T(8,128)(2,1)S(1)}, bf16[16,240,128]{2,1,0:T(8,128)(2,1)}) custom-call(bf16[240,2048]{1,0:T(8,128)(2,1)S(1)} %fusion.82.x_ref, bf16[16,80,128]{2,1,0:T(8,128)(2,1)S(1)} %all-to-all-done.6.g_ref, bf16[16,80,128]{2,1,0:T(8,128)(2,1)} %get-tuple-element.11.o_ref, f32[1,2048]{1,0:T(1,128)S(1)} %get-tuple-element.14.l_ref, ...), custom_call_target="tpu_custom_call" | custom-call | flops 10737418240 | bytes 3932160 | tf_op jit(solution)/shard_map/attn_bwd/pallas_call | solution.py:170
  327.2 3.9 convolution_convert_fusion.1
  333.2 2.4 fusion.32
  337.0 2.7 collective-permute-start.8
  340.4 3.8 collective-permute-done.4
  345.1 4.3 all-to-all-start.7
  349.4 9.6 %collective-permute-done.8 = bf16[240,1152]{1,0:T(8,128)(2,1)} collective-permute-done((bf16[240,1152]{1,0:T(8,128)(2,1)S(1)}, bf16[240,1152]{1,0:T(8,128)(2,1)}, u32[]{:S(2)}, u32[]{:S(2)}) %collective-permute-start.8) | collective-permute-done | bytes 552992 | tf_op jit(solution)/shard_map/ppermute | solution.py:199
  360.2 3.4 fusion.42
  363.8 80.3 %all-gather.12.cloned.1.call-done = bf16[6016,1152]{1,0:T(8,128)(2,1)} async-done(((bf16[376,1152]{1,0:T(8,128)(2,1)}), bf16[6016,1152]{1,0:T(8,128)(2,1)}) %all-gather.12.cloned.1.call-update) | async-done | bytes 13860880 | tf_op jit(solution)/shard_map/all_gather | solution.py:290
  444.0 4.7 slice.464
  448.7 3.4 fusion.43
  452.2 2.8 slice.474
  458.9 5.5 %concatenate.94 = f32[216,1152]{1,0:T(8,128)S(1)} concatenate(f32[18,1152]{1,0:T(8,128)} %get-tuple-element.64, f32[18,1152]{1,0:T(8,128)} %get-tuple-element.63, f32[18,1152]{1,0:T(8,128)} %get-tuple-element.62, f32[18,1152]{1,0:T(8,128)} %get-tuple-element.61, f32[18,1152]{1,0:T(8,128)} %get-tuple-element.60, f32[18,1152]{1,0:T(8,128)S(1)} %get-tuple-element.59, ...), dimensions={0} | concatenate | bytes 1990656 | tf_op jit(solution)/shard_map/concatenate | solution.py:247
  465.4 3.1 collective-permute-start.12
  469.5 4.6 collective-permute-done.12
  474.2 4.3 convolution_bitcast_fusion.1
  478.5 10.8 %collective-permute-done.10 = bf16[320,1152]{1,0:T(8,128)(2,1)S(1)} collective-permute-done((bf16[320,1152]{1,0:T(8,128)(2,1)S(1)}, bf16[320,1152]{1,0:T(8,128)(2,1)S(1)}, u32[]{:S(2)}, u32[]{:S(2)}) %collective-permute-start.10) | collective-permute-done | bytes 737312 | tf_op jit(solution)/shard_map/ppermute | solution.py:199
  490.3 3.8 concatenate.96
  496.5 3.6 fusion.183
  (190 shorter events, 51.3 us)
Async XLA Ops:
  7.2 62.7 %all-gather.8.cloned.1.call-start = ((), (), s32[]{:S(2)}) async-start(), calls=%async_computation.8 | async-start | bytes 5013504 | tf_op jit(solution)/shard_map/all_gather | solution.py:290
  8.7 155.6 %copy-start.20 = (f32[1152]{0:T(1024)}, f32[1152]{0:T(1024)S(1)}, u32[]{:S(2)}) copy-start(f32[1152]{0:T(1024)S(1)} %get-tuple-element.30) | copy-start | bytes 13828
  8.7 169.7 %copy-start.23 = (f32[1152]{0:T(1024)}, f32[1152]{0:T(1024)S(1)}, u32[]{:S(2)}) copy-start(f32[1152]{0:T(1024)S(1)} %get-tuple-element.35) | copy-start | bytes 13828
  8.7 7.1 %copy-start.15 = (bf16[1,2,1,72,1152]{4,3,2,1,0:T(8,128)(2,1)S(1)}, bf16[1,2,1,72,1152]{4,3,2,1,0:T(8,128)(2,1)}, u32[]{:S(2)}) copy-start(bf16[1,2,1,72,1152]{4,3,2,1,0:T(8,128)(2,1)} %param.11) | copy-start | bytes 995332
  9.8 6.0 %copy-start.25 = (f32[128]{0:T(128)}, f32[128]{0:T(128)S(1)}, u32[]{:S(2)}) copy-start(f32[128]{0:T(128)S(1)} %broadcast_multiply_fusion.9) | copy-start | bytes 1540
  11.0 4.8 copy-start.29
  13.0 125.6 %all-gather.10.cloned.1.call-start = ((), (), s32[]{:S(2)}) async-start(), calls=%async_computation.9 | async-start | bytes 7833600 | tf_op jit(solution)/shard_map/all_gather | solution.py:290
  14.7 11.9 %copy-start.33 = (s32[1,2]{1,0:T(1,128)S(1)}, s32[1,2]{1,0:T(1,128)}, u32[]{:S(2)}) copy-start(s32[1,2]{1,0:T(1,128)} %param.13) | copy-start | bytes 28
  17.3 15.6 %all-to-all-start = ((s32[16,1,128]{2,1,0:T(1,128)}), s32[16,1,128]{2,1,0:T(1,128)S(1)}, u32[]{:S(2)}, u32[]{:S(2)}) async-start(s32[16,1,128]{2,1,0:T(1,128)} %broadcast_in_dim.23), calls=%async_computation | async-start | bytes 16384 | tf_op jit(solution)/shard_map/all_to_all | solution.py:209
  26.6 47.1 %copy-start.17 = (bf16[240,1152]{1,0:T(8,128)(2,1)}, bf16[240,1152]{1,0:T(8,128)(2,1)S(1)}, u32[]{:S(2)}) copy-start(bf16[240,1152]{1,0:T(8,128)(2,1)S(1)} %pad_dynamic-update-slice_fusion.1) | copy-start | bytes 1658884
  146.5 31.9 %collective-permute-start = (bf16[16,40,1152]{2,1,0:T(8,128)(2,1)S(1)}, bf16[16,40,1152]{2,1,0:T(8,128)(2,1)}, u32[]{:S(2)}, u32[]{:S(2)}) collective-permute-start(bf16[16,40,1152]{2,1,0:T(8,128)(2,1)S(1)} %get-tuple-element.44), channel_id=1, source_target_pairs={{0,32},{32,0},{64,96},{96,64},{1,33},{33,1},{65,97},{97,65},{2,34}... | collective-permute-start | bytes 4423688 | tf_op jit(solution)/shard_map/ppermute | solution.py:199
  146.5 51.1 %collective-permute-start.2 = (bf16[16,120,1152]{2,1,0:T(8,128)(2,1)}, bf16[16,120,1152]{2,1,0:T(8,128)(2,1)}, u32[]{:S(2)}, u32[]{:S(2)}) collective-permute-start(bf16[16,120,1152]{2,1,0:T(8,128)(2,1)} %slice.449), channel_id=1, source_target_pairs={{0,32},{32,0},{64,96},{96,64},{1,33},{33,1},{65,97},{97,65},{2,34}... | collective-permute-start | bytes 13271048 | tf_op jit(solution)/shard_map/ppermute | solution.py:199
  148.1 16.2 %copy-start.35 = (bf16[1,128,1152]{2,1,0:T(8,128)(2,1)S(1)}, bf16[1,128,1152]{2,1,0:T(8,128)(2,1)}, u32[]{:S(2)}) copy-start(bf16[1,128,1152]{2,1,0:T(8,128)(2,1)} %param.15) | copy-start | bytes 884740
  148.1 38.3 %collective-permute-start.3 = (bf16[16,40,1152]{2,1,0:T(8,128)(2,1)}, bf16[16,40,1152]{2,1,0:T(8,128)(2,1)}, u32[]{:S(2)}, u32[]{:S(2)}) collective-permute-start(bf16[16,40,1152]{2,1,0:T(8,128)(2,1)} %get-tuple-element.43), channel_id=1, source_target_pairs={{0,32},{32,0},{64,96},{96,64},{1,33},{33,1},{65,97},{97,65},{2,34}... | collective-permute-start | bytes 4423688 | tf_op jit(solution)/shard_map/ppermute | solution.py:199
  158.9 15.4 %all-to-all-start.1 = ((bf16[16,80,128]{2,1,0:T(8,128)(2,1)}), bf16[16,80,128]{2,1,0:T(8,128)(2,1)}, u32[]{:S(2)}, u32[]{:S(2)}) async-start(bf16[16,80,128]{2,1,0:T(8,128)(2,1)} %get-tuple-element.11.o_ref), calls=%async_computation.1 | async-start | bytes 655360 | tf_op jit(solution)/shard_map/all_to_all | solution.py:209
  167.9 10.5 %copy-start = (bf16[1,1,128,1152]{3,2,1,0:T(8,128)(2,1)S(1)}, bf16[1,1,128,1152]{3,2,1,0:T(8,128)(2,1)}, u32[]{:S(2)}) copy-start(bf16[1,1,128,1152]{3,2,1,0:T(8,128)(2,1)} %param.8) | copy-start | bytes 884740
  180.4 6.0 %copy-start.16 = (bf16[128,1152]{1,0:T(8,128)(2,1)S(1)}, bf16[128,1152]{1,0:T(8,128)(2,1)}, u32[]{:S(2)}) copy-start(bf16[128,1152]{1,0:T(8,128)(2,1)} %get-tuple-element.101) | copy-start | bytes 884740
  182.9 10.5 %copy-start.18 = (f32[1152]{0:T(1024)S(1)}, f32[1152]{0:T(1024)}, u32[]{:S(2)}) copy-start(f32[1152]{0:T(1024)} %get-tuple-element.32) | copy-start | bytes 13828
  182.9 10.5 %copy-start.22 = (f32[1152]{0:T(1024)S(1)}, f32[1152]{0:T(1024)}, u32[]{:S(2)}) copy-start(f32[1152]{0:T(1024)} %get-tuple-element.31) | copy-start | bytes 13828
  182.9 10.1 %collective-permute-start.1 = (bf16[128,1152]{1,0:T(8,128)(2,1)S(1)}, bf16[128,1152]{1,0:T(8,128)(2,1)S(1)}, u32[]{:S(2)}, u32[]{:S(2)}) collective-permute-start(bf16[128,1152]{1,0:T(8,128)(2,1)S(1)} %fusion.29), channel_id=1, source_target_pairs={{0,16},{1,17},{2,18},{3,19},{4,20},{5,21},{6,22},{7,23},{8,24},{9,... | collective-permute-start | bytes 884744 | tf_op jit(solution)/shard_map/ppermute | solution.py:205
  189.2 15.8 %all-to-all-start.3 = ((bf16[16,80,128]{2,1,0:T(8,128)(2,1)}), bf16[16,80,128]{2,1,0:T(8,128)(2,1)S(1)}, u32[]{:S(2)}, u32[]{:S(2)}) async-start(bf16[16,80,128]{2,1,0:T(8,128)(2,1)} %pad_maximum_fusion.3), calls=%async_computation.3 | async-start | bytes 655360 | tf_op jit(solution)/shard_map/all_to_all | solution.py:209
  192.7 167.5 %all-gather.14.cloned.1.call-start = ((), (), s32[]{:S(2)}) async-start(), calls=%async_computation.11 | async-start | bytes 5013504 | tf_op jit(solution)/shard_map/all_gather | solution.py:290
  193.0 4.5 copy-start.8
  193.2 4.3 copy-start.27
  193.4 4.1 copy-start.31
  205.0 61.2 %slice-start = ((s8[7372800]{0:T(1024)(128)(4,1)}), s8[4194304]{0:T(1024)(128)(4,1)S(1)}, s32[]{:S(2)}) async-start(s8[7372800]{0:T(1024)(128)(4,1)} %bitcast.231), calls=%async_computation.12 | async-start | bytes 8388608
  227.8 38.4 %slice-start.1 = ((s8[7372800]{0:T(1024)(128)(4,1)}), s8[3178496]{0:T(1024)(128)(4,1)S(1)}, s32[]{:S(2)}) async-start(s8[7372800]{0:T(1024)(128)(4,1)} %bitcast.231), calls=%async_computation.13 | async-start | bytes 6356992
  266.2 13.7 %slice-start.2 = ((s8[5308416]{0:T(1024)(128)(4,1)}), s8[4194304]{0:T(1024)(128)(4,1)S(1)}, s32[]{:S(2)}) async-start(s8[5308416]{0:T(1024)(128)(4,1)} %bitcast.244), calls=%async_computation.14 | async-start | bytes 8388608
  267.1 12.7 %slice-start.3 = ((s8[5308416]{0:T(1024)(128)(4,1)}), s8[1114112]{0:T(1024)(128)(4,1)S(1)}, s32[]{:S(2)}) async-start(s8[5308416]{0:T(1024)(128)(4,1)} %bitcast.244), calls=%async_computation.15 | async-start | bytes 2228224
  270.9 9.0 %copy-start.24 = (f32[1152]{0:T(1024)S(1)}, f32[1152]{0:T(1024)}, u32[]{:S(2)}) copy-start(f32[1152]{0:T(1024)} %copy-done.23) | copy-start | bytes 13828
  270.9 9.0 %copy-start.36 = (bf16[1,128,1152]{2,1,0:T(8,128)(2,1)S(1)}, bf16[1,128,1152]{2,1,0:T(8,128)(2,1)}, u32[]{:S(2)}) copy-start(bf16[1,128,1152]{2,1,0:T(8,128)(2,1)} %param.15) | copy-start | bytes 884740
  271.3 8.6 %collective-permute-start.5 = (bf16[128,1152]{1,0:T(8,128)(2,1)S(1)}, bf16[128,1152]{1,0:T(8,128)(2,1)S(1)}, u32[]{:S(2)}, u32[]{:S(2)}) collective-permute-start(bf16[128,1152]{1,0:T(8,128)(2,1)S(1)} %get-tuple-element.36), channel_id=1, source_target_pairs={{16,0},{17,1},{18,2},{19,3},{20,4},{21,5},{22,6},{23,7},{24,8},{25... | collective-permute-start | bytes 884744 | tf_op jit(solution)/shard_map/ppermute | solution.py:205
  281.8 162.2 %all-gather.12.cloned.1.call-start = ((), (), s32[]{:S(2)}) async-start(), calls=%async_computation.10 | async-start | bytes 14727168 | tf_op jit(solution)/shard_map/all_gather | solution.py:290
  284.9 14.7 %all-to-all-start.4 = ((bf16[16,80,128]{2,1,0:T(8,128)(2,1)}), bf16[16,80,128]{2,1,0:T(8,128)(2,1)S(1)}, u32[]{:S(2)}, u32[]{:S(2)}) async-start(bf16[16,80,128]{2,1,0:T(8,128)(2,1)} %get-tuple-element.12), calls=%async_computation.4 | async-start | bytes 655360 | tf_op jit(solution)/shard_map/all_to_all | solution.py:209
  300.3 12.6 %all-to-all-start.6 = ((bf16[16,80,128]{2,1,0:T(8,128)(2,1)}), bf16[16,80,128]{2,1,0:T(8,128)(2,1)S(1)}, u32[]{:S(2)}, u32[]{:S(2)}) async-start(bf16[16,80,128]{2,1,0:T(8,128)(2,1)} %pad_maximum_fusion.4), calls=%async_computation.6 | async-start | bytes 655360 | tf_op jit(solution)/shard_map/all_to_all | solution.py:209
  327.2 4.1 copy-start.5
  327.2 4.1 copy-start.7
  327.2 4.1 copy-start.21
  331.2 5.7 %collective-permute-start.7 = (bf16[240,1152]{1,0:T(8,128)(2,1)S(1)}, bf16[240,1152]{1,0:T(8,128)(2,1)S(1)}, u32[]{:S(2)}, u32[]{:S(2)}) collective-permute-start(bf16[240,1152]{1,0:T(8,128)(2,1)S(1)} %convolution_convert_fusion.1), channel_id=1, source_target_pairs={{0,32},{32,0},{64,96},{96,64},{1,33},{33,1},{65,97},{97,65},{2,34}... | collective-permute-start | bytes 1658888 | tf_op jit(solution)/shard_map/ppermute | solution.py:199
  333.1 11.1 %copy-start.9 = (bf16[128,1152]{1,0:T(8,128)(2,1)S(1)}, bf16[128,1152]{1,0:T(8,128)(2,1)}, u32[]{:S(2)}) copy-start(bf16[128,1152]{1,0:T(8,128)(2,1)} %copy-done.8) | copy-start | bytes 884740
  335.5 8.7 %collective-permute-start.4 = (bf16[128,1152]{1,0:T(8,128)(2,1)S(1)}, bf16[128,1152]{1,0:T(8,128)(2,1)S(1)}, u32[]{:S(2)}, u32[]{:S(2)}) collective-permute-start(bf16[128,1152]{1,0:T(8,128)(2,1)S(1)} %fusion.32), channel_id=1, source_target_pairs={{0,16},{1,17},{2,18},{3,19},{4,20},{5,21},{6,22},{7,23},{8,24},{9,... | collective-permute-start | bytes 884744 | tf_op jit(solution)/shard_map/ppermute | solution.py:205
  337.0 22.0 %collective-permute-start.8 = (bf16[240,1152]{1,0:T(8,128)(2,1)S(1)}, bf16[240,1152]{1,0:T(8,128)(2,1)}, u32[]{:S(2)}, u32[]{:S(2)}) collective-permute-start(bf16[240,1152]{1,0:T(8,128)(2,1)S(1)} %add_convert_fusion.1), channel_id=1, source_target_pairs={{0,64},{32,96},{64,0},{96,32},{1,65},{33,97},{65,1},{97,33},{2,66}... | collective-permute-start | bytes 1658888 | tf_op jit(solution)/shard_map/ppermute | solution.py:199
  345.1 129.1 %all-to-all-start.7 = ((bf16[16,240,128]{2,1,0:T(8,128)(2,1)}), bf16[16,240,128]{2,1,0:T(8,128)(2,1)}, u32[]{:S(2)}, u32[]{:S(2)}) async-start(bf16[16,240,128]{2,1,0:T(8,128)(2,1)} %get-tuple-element.15), calls=%async_computation.7 | async-start | bytes 1966080 | tf_op jit(solution)/shard_map/all_to_all | solution.py:209
  363.7 100.7 %collective-permute-start.11 = (bf16[80,1152]{1,0:T(8,128)(2,1)S(1)}, bf16[80,1152]{1,0:T(8,128)(2,1)}, u32[]{:S(2)}, u32[]{:S(2)}) collective-permute-start(bf16[80,1152]{1,0:T(8,128)(2,1)S(1)} %fusion.42), channel_id=1, source_target_pairs={{0,32},{32,0},{64,96},{96,64},{1,33},{33,1},{65,97},{97,65},{2,34}... | collective-permute-start | bytes 552968 | tf_op jit(solution)/shard_map/ppermute | solution.py:199
  455.0 41.5 %collective-permute-start.6 = (bf16[16,120,1152]{2,1,0:T(8,128)(2,1)}, bf16[16,120,1152]{2,1,0:T(8,128)(2,1)}, u32[]{:S(2)}, u32[]{:S(2)}) collective-permute-start(bf16[16,120,1152]{2,1,0:T(8,128)(2,1)} %slice.464), channel_id=1, source_target_pairs={{0,32},{32,0},{64,96},{96,64},{1,33},{33,1},{65,97},{97,65},{2,34}... | collective-permute-start | bytes 13271048 | tf_op jit(solution)/shard_map/ppermute | solution.py:199
  457.5 10.9 %collective-permute-start.9 = (bf16[320,1152]{1,0:T(8,128)(2,1)}, bf16[320,1152]{1,0:T(8,128)(2,1)S(1)}, u32[]{:S(2)}, u32[]{:S(2)}) collective-permute-start(bf16[320,1152]{1,0:T(8,128)(2,1)} %pad_maximum_fusion.1), channel_id=1, source_target_pairs={{0,32},{32,0},{64,96},{96,64},{1,33},{33,1},{65,97},{97,65},{2,34}... | collective-permute-start | bytes 2211848 | tf_op jit(solution)/shard_map/ppermute | solution.py:199
  465.4 8.8 %collective-permute-start.12 = (bf16[80,1152]{1,0:T(8,128)(2,1)S(1)}, bf16[80,1152]{1,0:T(8,128)(2,1)S(1)}, u32[]{:S(2)}, u32[]{:S(2)}) collective-permute-start(bf16[80,1152]{1,0:T(8,128)(2,1)S(1)} %add_convert_fusion.3), channel_id=1, source_target_pairs={{0,64},{32,96},{64,0},{96,32},{1,65},{33,97},{65,1},{97,33},{2,66}... | collective-permute-start | bytes 552968 | tf_op jit(solution)/shard_map/ppermute | solution.py:199
  468.7 20.7 %collective-permute-start.10 = (bf16[320,1152]{1,0:T(8,128)(2,1)S(1)}, bf16[320,1152]{1,0:T(8,128)(2,1)S(1)}, u32[]{:S(2)}, u32[]{:S(2)}) collective-permute-start(bf16[320,1152]{1,0:T(8,128)(2,1)S(1)} %add_convert_fusion), channel_id=1, source_target_pairs={{0,64},{32,96},{64,0},{96,32},{1,65},{33,97},{65,1},{97,33},{2,66}... | collective-permute-start | bytes 2211848 | tf_op jit(solution)/shard_map/ppermute | solution.py:199
  (16 other events, 39.0 us)
Sparse Core Ops, SparseCore 0:
  13.1 56.6 all-gather.7
  72.5 66.0 all-gather.9
  281.9 53.3 all-gather.13
  337.3 106.6 all-gather.11
